TPU v7x, 256 devices: a whole 4x4x8 slice. The times are simulated.
256 devices in a mesh: energy: 64 (over z, y, core), slab: 4 (over x).
Axes of the slice: x: 4, y: 4, z: 8, core: 2. Of those that a mesh axis runs over, the one named last changes fastest.
Arguments:
- inv_diag: bfloat16 [2, 128, 16, 128, 128], P(None, 'energy', 'slab'), may hold values from -2 to 2, as said below
- coupling: bfloat16 [16, 128, 128], P('slab'), may hold values from -1 to 1
- tile_rows: int32 [16, 16], P('slab'), may hold values from 0 to 127, as said below
- tile_count: int32 [16], P('slab'), may hold values from 1 to 16, 160 in all
- kernel: bfloat16 [2, 255], replicated, may hold values from -0.5 to 0.5
Outputs:
- g_diag: float32 [2, 128, 16, 128, 128], P(None, 'energy', 'slab')
- self_energy: bfloat16 [2, 128, 16, 16, 128], P(None, 'energy', 'slab')
Inputs may be any that keep to these rules, and one draw needn't show every extreme that they name: `inv_diag`: complex blocks with a diagonal part and full off-diagonal entries. `tile_rows`: within one slab the 16 entries are distinct. `tile_count`: the counts add up to 160.
All inputs are finite; a program needn't handle non-finite values. No bound on the sum of `tile_count` on one device may be relied on, other than what follows from the above.
Results may differ from a plain program's by a relative error of at most 0.0057.
Values may be sent and summed in bfloat16 or wider, within the bound.
A program may use at most 64 MiB of HBM per device.

v0:
```python
import functools

import jax
import jax.numpy as jnp
from jax import lax
from jax.experimental import pallas as pl
from jax.experimental.pallas import tpu as pltpu
from jax.sharding import PartitionSpec as P

MESH = pl.DeviceIdType.MESH
F32 = jnp.float32
BF16 = jnp.bfloat16


def mm(a, b):
    return lax.dot_general(a, b, (((1,), (0,)), ((), ())), preferred_element_type=F32)


def mm_t(a, b):
    return lax.dot_general(a, b, (((1,), (1,)), ((), ())), preferred_element_type=F32)


def stacked(real, imag):
    return jnp.concatenate([real, imag], 0).astype(BF16)


def beside(real, imag):
    return jnp.concatenate([real, imag], 1).astype(BF16)


def cross(x):
    h, w = x.shape[0] // 2, x.shape[1] // 2
    return x[:h, :w] - x[h:, w:], x[:h, w:] + x[h:, :w]


def times(left_stacked, right_beside):
    return cross(mm(left_stacked, right_beside))


def times_t(real, imag, right_stacked):
    return cross(mm_t(stacked(real, imag), right_stacked))


def around(outer_stacked, middle_beside):
    return times_t(*times(outer_stacked, middle_beside), outer_stacked)


def peer_order():
    offsets = [
        (min(dz, 8 - dz) + min(dy, 4 - dy), dc, dz, dy)
        for dz in range(8)
        for dy in range(4)
        for dc in range(2)
        if dz or dy or dc
    ]
    return sorted(offsets, reverse=True)


def rows_of(slab, part, q):
    return pl.ds(64 * slab + 2 * part + q, 8, stride=8)


def kernel(
    d_hbm,
    coupling_hbm,
    rows_hbm,
    count_hbm,
    conv_hbm,
    g_out,
    in_2,
    d,
    coupling,
    rows_ref,
    count_ref,
    conv_ref,
    acc,
    walk,
    product,
    end,
    into,
    relay,
    far_end,
    far_walk,
    conv_pad,
    conv_mat,
    pick,
    pick_walk,
    base,
    stage,
    out_1,
    in_1,
    out_2,
    arrived,
    answer,
    load_sem,
    chain_send,
    chain_recv,
    a2a_send,
    a2a_recv,
    lines_here,
    columns_here,
    ready,
):
    me = lax.axis_index("energy")
    slab = lax.axis_index("slab")
    peers = lax.axis_size("energy")
    n_e, n_s, orb = d.shape[1], d.shape[2], d.shape[3]
    slots = n_s * 16
    last = n_s - 1

    coupling_load = pltpu.make_async_copy(coupling_hbm, coupling, load_sem.at[0])
    slab_loads = [
        pltpu.make_async_copy(d_hbm.at[:, :, i], d.at[:, :, i], load_sem.at[1 + i])
        for i in range(n_s)
    ]
    small_loads = [
        pltpu.make_async_copy(rows_hbm, rows_ref, load_sem.at[1 + n_s]),
        pltpu.make_async_copy(count_hbm, count_ref, load_sem.at[2 + n_s]),
        pltpu.make_async_copy(conv_hbm, conv_ref, load_sem.at[3 + n_s]),
    ]
    for c in [coupling_load, slab_loads[1], slab_loads[0]] + slab_loads[2:] + small_loads:
        c.start()

    barrier = pltpu.get_barrier_semaphore()

    z, y, core = lax.div(me, 8), lax.rem(lax.div(me, 2), 4), lax.rem(me, 2)

    def others():
        for _, dc, dz, dy in peer_order():
            there = lax.rem(core + dc, 2)
            yield lax.rem(z + dz, 8) * 8 + lax.rem(y + dy, 4) * 2 + there

    for receiver, sender in ((1, 0), (2, 1), (3, 1), (3, 2), (0, 1), (2, 3)):

        @pl.when(slab == receiver)
        def _():
            pl.semaphore_signal(
                barrier, inc=1, device_id={"slab": sender}, device_id_type=MESH
            )

    odd = lax.rem(slab, 2) == 1

    def greet(semaphore, j):
        pl.semaphore_signal(semaphore, inc=1, device_id={"energy": j}, device_id_type=MESH)

    column = [lax.rem(z + k, 8) * 8 + lax.rem(me, 8) for k in (4, 3, 5, 2, 6, 1, 7)]
    plane = [z * 8 + lax.rem(lax.rem(me, 8) + k, 8) for k in range(1, 8)]

    @pl.when(odd)
    def _():
        for j in column + plane:
            greet(barrier, j)


    def coupled(i):
        x = mm(d[:, :, i].reshape(2 * n_e * orb, orb), coupling[i]).astype(BF16)
        x = x.reshape(2, n_e, orb, orb)
        return [x[:, e].reshape(2 * orb, orb) for e in range(n_e)]

    every = range(n_e)

    coupling_load.wait()
    slab_loads[1].wait()
    step = [None, coupled(1)]
    slab_loads[0].wait()
    now = [beside(d[0, e, 0], d[1, e, 0]) for e in every]

    def plus(e, i, moved):
        return [d[c, e, i].astype(F32) + moved[c] for c in range(2)]

    def keep(e, i, new):
        for c in range(2):
            acc[e, i, c] = new[c]

    second = [plus(e, 1, around(step[1][e], now[e])) for e in every]
    slab_loads[2].wait()
    step.append(coupled(2))
    slab_loads[3].wait()
    step.append(coupled(3))
    both = [
        stacked(*times(step[3][e], beside(step[2][e][:orb], step[2][e][orb:]))) for e in every
    ]
    outer = [plus(e, 3, around(step[3][e], beside(d[0, e, 2], d[1, e, 2]))) for e in every]
    for e in every:
        keep(e, 1, second[e])
        moved = around(both[e], beside(*second[e]))
        new = [outer[e][c] + moved[c] for c in range(2)]
        keep(e, 3, new)
        end[e] = beside(*new)

    around_here = len(column) + len(plane)
    first = jnp.where(odd, jnp.where(slab == 3, 1, 3) + around_here, 1)
    pl.semaphore_wait(barrier, first)

    @pl.when(odd)
    def _():
        for j in column:
            greet(lines_here, j)

    def push(src, dst, send, recv, to):
        return pltpu.make_async_remote_copy(
            src, dst, send, recv, device_id={"slab": to}, device_id_type=MESH
        )

    first_hop = [
        push(end.at[e], into.at[e], chain_send.at[e], chain_recv.at[e], 1)
        for e in range(n_e)
    ]
    far_hop = [
        (
            push(end.at[e], far_end.at[e], chain_send.at[e], chain_recv.at[2 + e], 3),
            push(product.at[e], far_walk.at[e], chain_send.at[2 + e], chain_recv.at[4 + e], 3),
        )
        for e in range(n_e)
    ]
    second_hop = [
        [
            push(relay.at[e], into.at[e], chain_send.at[2 * e + j], chain_recv.at[e], 2 + j)
            for j in range(2)
        ]
        for e in range(n_e)
    ]

    @pl.when(slab == 0)
    def _():
        for c in first_hop:
            c.start()

    @pl.when(slab == 2)
    def _():
        for pair in far_hop:
            pair[0].start()

    step[0] = coupled(0)
    for e in every:
        walk[e, 0] = step[0][e]
        now[e] = beside(step[0][e][:orb], step[0][e][orb:])
    for i in range(1, n_s):
        for e in every:
            moved = times(step[i][e], now[e])
            walk[e, i] = stacked(*moved)
            now[e] = beside(*moved)
            if i == last:
                product[e] = now[e]

    @pl.when(slab == 2)
    def _():
        for pair in far_hop:
            pair[1].start()

    for e in every:
        for c in range(2):
            acc[e, 0, c] = d[c, e, 0].astype(F32)
        keep(e, 2, plus(e, 2, around(step[2][e], beside(acc[e, 1, 0], acc[e, 1, 1]))))

    for c in small_loads:
        c.wait()

    row_at = lax.broadcasted_iota(jnp.int32, (16, orb), 0)
    lane_at = lax.broadcasted_iota(jnp.int32, (16, orb), 1)
    for i in range(n_s):
        wanted = jnp.full((16, orb), -1, jnp.int32)
        for t in range(16):
            row = jnp.where(t < count_ref[i], rows_ref[i, t], -1)
            wanted = jnp.where(row_at == t, row, wanted)
        pick[i] = jnp.where(lane_at == wanted, 1.0, 0.0).astype(BF16)

    conv_pad[...] = jnp.zeros_like(conv_pad)
    conv_pad[0:2, 0 : 2 * orb - 1] = conv_ref[...].astype(F32)
    bands = []
    for c in range(2):
        wide = jnp.broadcast_to(conv_pad[c : c + 1, :], (orb, 2 * orb))
        bands.append(pltpu.roll(wide, orb + 1, 1, stride=1, stride_axis=0)[:, :orb])
    flipped = jnp.concatenate(
        [
            jnp.concatenate([bands[0], bands[1]], 1),
            jnp.concatenate([-bands[1], bands[0]], 1),
        ],
        0,
    ).astype(BF16)
    big = (2 * orb, 2 * orb)
    row_at = lax.broadcasted_iota(jnp.int32, big, 0)
    lane_at = lax.broadcasted_iota(jnp.int32, big, 1)
    order = jnp.where(
        lane_at == lax.rem(row_at, 2) * orb + lax.div(row_at, 2), 1.0, 0.0
    ).astype(BF16)
    conv_mat[...] = mm_t(order, mm(order, flipped).astype(BF16)).astype(BF16)

    for e in every:
        for i in range(n_s):
            at = slice(16 * i, 16 * i + 16)
            own = walk[e, i]
            chosen = mm(pick[i], jnp.concatenate([own[:orb], own[orb:]], 1)).astype(BF16)
            pick_walk[e, at] = chosen[:, :orb]
            pick_walk[e, slots + 16 * i : slots + 16 * i + 16] = chosen[:, orb:]
            high = beside(acc[e, i, 0], acc[e, i, 1])
            low = beside(*[acc[e, i, c] - acc[e, i, c].astype(BF16).astype(F32) for c in range(2)])
            base[e, at] = mm(pick[i], high) + mm(pick[i], low)

    def rows_around(e, middle):
        real, imag = times(pick_walk[e], middle)
        for i in range(n_s):
            at = slice(16 * i, 16 * i + 16)
            yield i, at, times_t(real[at], imag[at], walk[e, i])

    def blocks_around(e, middle):
        mid = mm(walk[e].reshape(n_s * 2 * orb, orb), middle).reshape(n_s, 2 * orb, 2 * orb)
        for i in range(n_s):
            yield i, times_t(*cross(mid[i]), walk[e, i])

    def select(e):
        for i, at, moved in rows_around(e, into[e]):
            for c in range(2):
                part = base[e, at, c * orb : (c + 1) * orb] + moved[c]
                for q in range(2):
                    stage[rows_of(i, 2 * e + c, q), :] = part[8 * q : 8 * q + 8]

    def lines_are_here():
        pl.semaphore_wait(lines_here, len(column))
        for j in plane:
            greet(columns_here, j)

    def all_here(to):
        pl.semaphore_wait(columns_here, len(plane))
        pl.semaphore_signal(ready, inc=1, device_id={"slab": to}, device_id_type=MESH)

    @pl.when(slab == 0)
    def _():
        into[...] = jnp.zeros_like(into)

    @pl.when(slab == 1)
    def _():
        for e in every:
            first_hop[e].wait_recv()
            moved = around(walk[e, last], into[e])
            relay[e] = beside(*[acc[e, last, c] + moved[c] for c in range(2)])
            for c in second_hop[e]:
                c.start()
            if e == 0:
                lines_are_here()
        all_here(0)

    @pl.when(slab == 3)
    def _():
        lines_are_here()
        for e in every:
            far_hop[e][0].wait_recv()
            for i, at, moved in rows_around(e, far_end[e]):
                base[e, at] = base[e, at] + jnp.concatenate(moved, 1)
            for i, moved in blocks_around(e, far_end[e]):
                for c in range(2):
                    acc[e, i, c] = acc[e, i, c] + moved[c]
        all_here(2)
        for e in every:
            far_hop[e][1].wait_recv()
            pick_walk[e] = stacked(*times(pick_walk[e], far_walk[e]))
            for i in range(n_s):
                walk[e, i] = stacked(*times(walk[e, i], far_walk[e]))

    for e in every:

        @pl.when(slab >= 2)
        def _():
            second_hop[e][0].wait_recv()

        select(e)

    half = peers // 2
    mine = lax.rem(me, half)

    def send(src, dst, at, to):
        pltpu.make_async_remote_copy(
            src,
            dst,
            a2a_send.at[at],
            a2a_recv.at[at],
            device_id={"energy": to},
            device_id_type=MESH,
        ).start()

    def all_but_own(ref, count, sem):
        most = ref.at[pl.ds(0, count - 1)]
        return pltpu.make_async_copy(most, most, sem)

    out_1[...] = stage[...].astype(BF16).reshape(out_1.shape)

    @pl.when(jnp.logical_not(odd))
    def _():
        pl.semaphore_wait(ready, 1)

    for j in others():
        send(out_1.at[lax.rem(j, half)], in_1.at[me], 0, j)
    in_1[me] = out_1[mine]

    for e in every:
        for i, moved in blocks_around(e, into[e]):
            for c in range(2):
                g_out[c, e, i] = acc[e, i, c] + moved[c]

    all_but_own(in_1, peers, a2a_recv.at[0]).wait()
    arrived[...] = in_1[...].reshape(arrived.shape).astype(F32)
    for q in range(2):
        at = pl.ds(q, 4 * peers, stride=2)
        answer[at, :] = mm(conv_mat[...], arrived[at, :].astype(BF16))
    out_2[...] = answer[...].astype(BF16).reshape(out_2.shape)
    for dz in (2, 7, 1, 0):
        for dy in (2, 1, 3, 0):
            for dc in (1, 0):
                if dz or dy or dc:
                    there = lax.rem(y + dy, 4) * 2 + lax.rem(core + dc, 2)
                    j = lax.rem(z + dz, 8) * 8 + there
                    send(out_2.at[j], in_2.at[mine], 1, j)
    in_2[mine] = out_2[me]

    @pl.when(slab == 0)
    def _():
        for c in first_hop:
            c.wait_send()

    @pl.when(slab == 1)
    def _():
        for pair in second_hop:
            for c in pair:
                c.wait_send()

    @pl.when(slab == 2)
    def _():
        for pair in far_hop:
            for c in pair:
                c.wait_send()

    all_but_own(in_1, peers, a2a_send.at[0]).wait()
    all_but_own(in_2, half, a2a_recv.at[1]).wait()
    all_but_own(out_2, half, a2a_send.at[1]).wait()


def finish(g, rows, g_hbm, self_hbm, stage, self_out, sem):
    copies = [
        pltpu.make_async_copy(g, g_hbm, sem.at[0]),
        pltpu.make_async_copy(self_out, self_hbm, sem.at[1]),
    ]
    copies[0].start()
    _, n_e, n_s, _, orb = self_out.shape
    stage[...] = rows[...].reshape(stage.shape).astype(F32)
    for e in range(n_e):
        for c in range(2):
            for i in range(n_s):
                parts = [stage[rows_of(i, 2 * e + c, q), :] for q in range(2)]
                self_out[c, e, i] = jnp.concatenate(parts, 0).astype(BF16)
    copies[1].start()
    for c in copies:
        c.wait()


def on_device(inv_diag, coupling, tile_rows, tile_count, conv):
    _, n_e, n_s, orb, _ = inv_diag.shape
    slots = n_s * 16
    vmem = pl.BlockSpec(memory_space=pltpu.VMEM)
    dma = pltpu.SemaphoreType.DMA
    hbm = pl.BlockSpec(memory_space=pltpu.HBM)
    g_shape = jax.ShapeDtypeStruct(inv_diag.shape, F32)
    self_shape = jax.ShapeDtypeStruct((2, n_e, n_s, 16, orb), BF16)
    peers = lax.axis_size("energy")
    rows_shape = jax.ShapeDtypeStruct((slots // 2, 8, orb), BF16)
    g, rows = pl.pallas_call(
        kernel,
        out_shape=(g_shape, rows_shape),
        in_specs=[hbm] * 5,
        out_specs=(vmem, vmem),
        scratch_shapes=[
            pltpu.VMEM(inv_diag.shape, BF16),
            pltpu.VMEM(coupling.shape, BF16),
            pltpu.SMEM(tile_rows.shape, jnp.int32),
            pltpu.SMEM(tile_count.shape, jnp.int32),
            pltpu.VMEM(conv.shape, BF16),
            pltpu.VMEM((n_e, n_s, 2, orb, orb), F32),
            pltpu.VMEM((n_e, n_s, 2 * orb, orb), BF16),
            pltpu.VMEM((n_e, orb, 2 * orb), BF16),
            pltpu.VMEM((n_e, orb, 2 * orb), BF16),
            pltpu.VMEM((n_e, orb, 2 * orb), BF16),
            pltpu.VMEM((n_e, orb, 2 * orb), BF16),
            pltpu.VMEM((n_e, orb, 2 * orb), BF16),
            pltpu.VMEM((n_e, orb, 2 * orb), BF16),
            pltpu.VMEM((8, 2 * orb), F32),
            pltpu.VMEM((2 * orb, 2 * orb), BF16),
            pltpu.VMEM((n_s, 16, orb), BF16),
            pltpu.VMEM((n_e, 2 * slots, orb), BF16),
            pltpu.VMEM((n_e, slots, 2 * orb), F32),
            pltpu.VMEM((4 * slots, orb), F32),
            pltpu.VMEM((slots // 2, 8, orb), BF16),
            pltpu.VMEM((peers, 8, orb), BF16),
            pltpu.VMEM((peers, 8, orb), BF16),
            pltpu.VMEM((8 * peers, orb), F32),
            pltpu.VMEM((8 * peers, orb), F32),
            dma((n_s + 4,)),
            dma((4,)),
            dma((6,)),
            dma((2,)),
            dma((2,)),
            pltpu.SemaphoreType.REGULAR,
            pltpu.SemaphoreType.REGULAR,
            pltpu.SemaphoreType.REGULAR,
        ],
        compiler_params=pltpu.CompilerParams(
            collective_id=0, has_side_effects=True, vmem_limit_bytes=20 * 1024 * 1024
        ),
        name="dyson",
    )(
        *[
            pltpu.with_memory_space_constraint(x, pltpu.HBM)
            for x in (inv_diag, coupling, tile_rows, tile_count, conv)
        ]
    )
    return pl.pallas_call(
        finish,
        out_shape=(g_shape, self_shape),
        in_specs=[vmem, vmem],
        out_specs=(hbm, hbm),
        scratch_shapes=[
            pltpu.VMEM((4 * slots, orb), F32),
            pltpu.VMEM(self_shape.shape, BF16),
            dma((2,)),
        ],
        compiler_params=pltpu.CompilerParams(vmem_limit_bytes=8 * 1024 * 1024),
        name="finish",
    )(g, rows)


def solution(mesh):
    placed = (
        P(None, "energy", "slab", None, None),
        P("slab", None, None),
        P("slab", None),
        P("slab"),
        P(),
    )
    return jax.shard_map(
        on_device,
        mesh=mesh,
        in_specs=placed,
        out_specs=(P(None, "energy", "slab", None, None), P(None, "energy", "slab", None, None)),
        check_vma=False,
    )
```

profile of v0, /device:TPU:7, one launch (start us, length us, event | category | flops | bytes accessed | tf_op | source)
XLA Modules:
  0.0 28.7 jit_solution(5379433291037564435)
XLA Ops:
  0.6 27.1 %dyson.1 = (f32[2,2,4,128,128]{4,3,2,1,0:T(8,128)S(1)}, bf16[32,8,128]{2,1,0:T(8,128)(2,1)S(1)}) custom-call(bf16[2,2,4,128,128]{4,3,2,1,0:T(8,128)(2,1)} %d_hbm.1, bf16[4,128,128]{2,1,0:T(8,128)(2,1)} %coupling_hbm.1, s32[4,16]{1,0:T(4,128)} %rows_hbm.1, s32[4]{0:T(128)} %count_hbm.1, bf16[2,255]{1,0:T(2,128)(2,1)} %conv_hbm.1), custom_call_target="tpu_custom_call" | custom-call | tf_op jit(solution)/shard_map/dyson/pallas_call | solution.py:465
  27.7 1.0 %finish.1 = (f32[2,2,4,128,128]{4,3,2,1,0:T(8,128)}, bf16[2,2,4,16,128]{4,3,2,1,0:T(8,128)(2,1)}) custom-call(f32[2,2,4,128,128]{4,3,2,1,0:T(8,128)S(1)} %get-tuple-element.4.g, bf16[32,8,128]{2,1,0:T(8,128)(2,1)S(1)} %get-tuple-element.5.rows), custom_call_target="tpu_custom_call" | custom-call | tf_op jit(solution)/shard_map/finish/pallas_call | solution.py:514
where the time goes:
time: 29 us; the launch traced here: 28.7 us
  Pallas kernels  28.1 us (97%)
  between operations  0.64 us (2%)
    pallas_call x1, Pallas kernels, on_device(): pl.pallas_call(kernel, out_shape=(g_shape, rows_shape), in_specs=[hbm] *...  27.1 us
    pallas_call x1, Pallas kernels, on_device(): pl.pallas_call(finish, out_shape=(g_shape, self_shape), in_specs=[vmem, v...  0.99 us

commit v1 on v0

--- a/solution.py
+++ b/solution.py
@@ -97,7 +97,6 @@
     chain_recv,
     a2a_send,
     a2a_recv,
-    lines_here,
     columns_here,
     ready,
 ):
@@ -146,11 +145,13 @@
     column = [lax.rem(z + k, 8) * 8 + lax.rem(me, 8) for k in (4, 3, 5, 2, 6, 1, 7)]
     plane = [z * 8 + lax.rem(lax.rem(me, 8) + k, 8) for k in range(1, 8)]
 
-    @pl.when(odd)
-    def _():
-        for j in column + plane:
-            greet(barrier, j)
-
+    for j in column + plane:
+        pl.semaphore_signal(
+            barrier,
+            inc=1,
+            device_id={"energy": j, "slab": 2 * lax.div(slab, 2) + 1},
+            device_id_type=MESH,
+        )
 
     def coupled(i):
         x = mm(d[:, :, i].reshape(2 * n_e * orb, orb), coupling[i]).astype(BF16)
@@ -188,14 +189,14 @@
         keep(e, 3, new)
         end[e] = beside(*new)
 
-    around_here = len(column) + len(plane)
+    around_here = 2 * (len(column) + len(plane))
     first = jnp.where(odd, jnp.where(slab == 3, 1, 3) + around_here, 1)
     pl.semaphore_wait(barrier, first)
 
     @pl.when(odd)
     def _():
-        for j in column:
-            greet(lines_here, j)
+        for j in plane:
+            greet(columns_here, j)
 
     def push(src, dst, send, recv, to):
         return pltpu.make_async_remote_copy(
@@ -284,7 +285,9 @@
     order = jnp.where(
         lane_at == lax.rem(row_at, 2) * orb + lax.div(row_at, 2), 1.0, 0.0
     ).astype(BF16)
-    conv_mat[...] = mm_t(order, mm(order, flipped).astype(BF16)).astype(BF16)
+    whole_mat = mm_t(order, mm(order, flipped).astype(BF16)).astype(BF16)
+    conv_mat[: 2 * orb] = whole_mat
+    conv_mat[2 * orb :] = whole_mat[:orb]
 
     for e in every:
         for i in range(n_s):
@@ -315,11 +318,6 @@
                 for q in range(2):
                     stage[rows_of(i, 2 * e + c, q), :] = part[8 * q : 8 * q + 8]
 
-    def lines_are_here():
-        pl.semaphore_wait(lines_here, len(column))
-        for j in plane:
-            greet(columns_here, j)
-
     def all_here(to):
         pl.semaphore_wait(columns_here, len(plane))
         pl.semaphore_signal(ready, inc=1, device_id={"slab": to}, device_id_type=MESH)
@@ -336,13 +334,11 @@
             relay[e] = beside(*[acc[e, last, c] + moved[c] for c in range(2)])
             for c in second_hop[e]:
                 c.start()
-            if e == 0:
-                lines_are_here()
         all_here(0)
 
     @pl.when(slab == 3)
     def _():
-        lines_are_here()
+        all_here(2)
         for e in every:
             far_hop[e][0].wait_recv()
             for i, at, moved in rows_around(e, far_end[e]):
@@ -350,7 +346,6 @@
             for i, moved in blocks_around(e, far_end[e]):
                 for c in range(2):
                     acc[e, i, c] = acc[e, i, c] + moved[c]
-        all_here(2)
         for e in every:
             far_hop[e][1].wait_recv()
             pick_walk[e] = stacked(*times(pick_walk[e], far_walk[e]))
@@ -399,9 +394,10 @@
 
     all_but_own(in_1, peers, a2a_recv.at[0]).wait()
     arrived[...] = in_1[...].reshape(arrived.shape).astype(F32)
+    own_rows = pl.ds(pl.multiple_of(lax.rem(z + 7, 8) * 32, 32), 2 * peers)
     for q in range(2):
-        at = pl.ds(q, 4 * peers, stride=2)
-        answer[at, :] = mm(conv_mat[...], arrived[at, :].astype(BF16))
+        moved = mm(conv_mat[own_rows, :], arrived[pl.ds(q, 4 * peers, stride=2), :].astype(BF16))
+        answer[pl.ds(q, 2 * peers, stride=2), :] = moved
     out_2[...] = answer[...].astype(BF16).reshape(out_2.shape)
     for dz in (2, 7, 1, 0):
         for dy in (2, 1, 3, 0):
@@ -409,8 +405,8 @@
                 if dz or dy or dc:
                     there = lax.rem(y + dy, 4) * 2 + lax.rem(core + dc, 2)
                     j = lax.rem(z + dz, 8) * 8 + there
-                    send(out_2.at[j], in_2.at[mine], 1, j)
-    in_2[mine] = out_2[me]
+                    send(out_2.at[(dz + 1) % 8 * 8 + there], in_2.at[mine], 1, j)
+    in_2[mine] = out_2[8 + lax.rem(me, 8)]
 
     @pl.when(slab == 0)
     def _():
@@ -482,22 +478,21 @@
             pltpu.VMEM((n_e, orb, 2 * orb), BF16),
             pltpu.VMEM((n_e, orb, 2 * orb), BF16),
             pltpu.VMEM((8, 2 * orb), F32),
-            pltpu.VMEM((2 * orb, 2 * orb), BF16),
+            pltpu.VMEM((3 * orb, 2 * orb), BF16),
             pltpu.VMEM((n_s, 16, orb), BF16),
             pltpu.VMEM((n_e, 2 * slots, orb), BF16),
             pltpu.VMEM((n_e, slots, 2 * orb), F32),
             pltpu.VMEM((4 * slots, orb), F32),
             pltpu.VMEM((slots // 2, 8, orb), BF16),
             pltpu.VMEM((peers, 8, orb), BF16),
-            pltpu.VMEM((peers, 8, orb), BF16),
+            pltpu.VMEM((peers // 2, 8, orb), BF16),
             pltpu.VMEM((8 * peers, orb), F32),
-            pltpu.VMEM((8 * peers, orb), F32),
+            pltpu.VMEM((4 * peers, orb), F32),
             dma((n_s + 4,)),
             dma((4,)),
             dma((6,)),
             dma((2,)),
             dma((2,)),
-            pltpu.SemaphoreType.REGULAR,
             pltpu.SemaphoreType.REGULAR,
             pltpu.SemaphoreType.REGULAR,
         ],

time: 29 us -> 28.7 us (0.990)
  no operation moved by 1% of the time
where the time goes in v1:
time: 28.7 us; the launch traced here: 28.6 us
  Pallas kernels  27.9 us (97%)
  between operations  0.64 us (2%)
    pallas_call x1, Pallas kernels, on_device(): pl.pallas_call(kernel, out_shape=(g_shape, rows_shape), in_specs=[hbm] *...  26.9 us
    pallas_call x1, Pallas kernels, on_device(): pl.pallas_call(finish, out_shape=(g_shape, self_shape), in_specs=[vmem, v...  0.99 us

profile of v1, /device:TPU:7, one launch (start us, length us, event | category | flops | bytes accessed | tf_op | source)
XLA Modules:
  0.0 28.6 jit_solution(4772888218867065445)
XLA Ops:
  0.6 26.9 %dyson.1 = (f32[2,2,4,128,128]{4,3,2,1,0:T(8,128)S(1)}, bf16[32,8,128]{2,1,0:T(8,128)(2,1)S(1)}) custom-call(bf16[2,2,4,128,128]{4,3,2,1,0:T(8,128)(2,1)} %d_hbm.1, bf16[4,128,128]{2,1,0:T(8,128)(2,1)} %coupling_hbm.1, s32[4,16]{1,0:T(4,128)} %rows_hbm.1, s32[4]{0:T(128)} %count_hbm.1, bf16[2,255]{1,0:T(2,128)(2,1)} %conv_hbm.1), custom_call_target="tpu_custom_call" | custom-call | tf_op jit(solution)/shard_map/dyson/pallas_call | solution.py:461
  27.6 1.0 %finish.1 = (f32[2,2,4,128,128]{4,3,2,1,0:T(8,128)}, bf16[2,2,4,16,128]{4,3,2,1,0:T(8,128)(2,1)}) custom-call(f32[2,2,4,128,128]{4,3,2,1,0:T(8,128)S(1)} %get-tuple-element.4.g, bf16[32,8,128]{2,1,0:T(8,128)(2,1)S(1)} %get-tuple-element.5.rows), custom_call_target="tpu_custom_call" | custom-call | tf_op jit(solution)/shard_map/finish/pallas_call | solution.py:509

commit v2 on v1

--- a/solution.py
+++ b/solution.py
@@ -394,19 +394,19 @@
 
     all_but_own(in_1, peers, a2a_recv.at[0]).wait()
     arrived[...] = in_1[...].reshape(arrived.shape).astype(F32)
-    own_rows = pl.ds(pl.multiple_of(lax.rem(z + 7, 8) * 32, 32), 2 * peers)
+    own_rows = pl.ds(pl.multiple_of(lax.rem(z + 6, 8) * 32, 32), 2 * peers)
     for q in range(2):
         moved = mm(conv_mat[own_rows, :], arrived[pl.ds(q, 4 * peers, stride=2), :].astype(BF16))
         answer[pl.ds(q, 2 * peers, stride=2), :] = moved
     out_2[...] = answer[...].astype(BF16).reshape(out_2.shape)
-    for dz in (2, 7, 1, 0):
+    for dz in (6, 1, 7, 0):
         for dy in (2, 1, 3, 0):
             for dc in (1, 0):
                 if dz or dy or dc:
                     there = lax.rem(y + dy, 4) * 2 + lax.rem(core + dc, 2)
                     j = lax.rem(z + dz, 8) * 8 + there
-                    send(out_2.at[(dz + 1) % 8 * 8 + there], in_2.at[mine], 1, j)
-    in_2[mine] = out_2[8 + lax.rem(me, 8)]
+                    send(out_2.at[(dz + 2) % 8 * 8 + there], in_2.at[mine], 1, j)
+    in_2[mine] = out_2[16 + lax.rem(me, 8)]
 
     @pl.when(slab == 0)
     def _():

time: 28.7 us -> 28.5 us (level)
  no operation moved by 1% of the time
where the time goes in v2:
time: 28.5 us; the launch traced here: 28.4 us
  Pallas kernels  27.8 us (98%)
  between operations  0.64 us (2%)
    pallas_call x1, Pallas kernels, on_device(): pl.pallas_call(kernel, out_shape=(g_shape, rows_shape), in_specs=[hbm] *...  26.8 us
    pallas_call x1, Pallas kernels, on_device(): pl.pallas_call(finish, out_shape=(g_shape, self_shape), in_specs=[vmem, v...  0.99 us

profile of v2, /device:TPU:7, one launch (start us, length us, event | category | flops | bytes accessed | tf_op | source)
XLA Modules:
  0.0 28.4 jit_solution(12975033469393031979)
XLA Ops:
  0.6 26.8 %dyson.1 = (f32[2,2,4,128,128]{4,3,2,1,0:T(8,128)S(1)}, bf16[32,8,128]{2,1,0:T(8,128)(2,1)S(1)}) custom-call(bf16[2,2,4,128,128]{4,3,2,1,0:T(8,128)(2,1)} %d_hbm.1, bf16[4,128,128]{2,1,0:T(8,128)(2,1)} %coupling_hbm.1, s32[4,16]{1,0:T(4,128)} %rows_hbm.1, s32[4]{0:T(128)} %count_hbm.1, bf16[2,255]{1,0:T(2,128)(2,1)} %conv_hbm.1), custom_call_target="tpu_custom_call" | custom-call | tf_op jit(solution)/shard_map/dyson/pallas_call | solution.py:461
  27.4 1.0 %finish.1 = (f32[2,2,4,128,128]{4,3,2,1,0:T(8,128)}, bf16[2,2,4,16,128]{4,3,2,1,0:T(8,128)(2,1)}) custom-call(f32[2,2,4,128,128]{4,3,2,1,0:T(8,128)S(1)} %get-tuple-element.4.g, bf16[32,8,128]{2,1,0:T(8,128)(2,1)S(1)} %get-tuple-element.5.rows), custom_call_target="tpu_custom_call" | custom-call | tf_op jit(solution)/shard_map/finish/pallas_call | solution.py:509
